TPU v7x, 32 devices: a whole 2x2x4 slice. The times are simulated.
32 devices in a mesh: groups: 2 (over y), site: 4 (over z), member: 4 (over x, core).
Axes of the slice: x: 2, y: 2, z: 4, core: 2. Of those that a mesh axis runs over, the one named last changes fastest.
Arguments:
- tokens: bfloat16 [2048, 2880], P(('groups', 'site', 'member')), parts along dimension 0, may hold values from -6 to 6
- expert_ids: int32 [2048, 4], P(('groups', 'site', 'member')), parts along dimension 0, may hold values from 0 to 15, as said below
- route_weights: bfloat16 [2048, 4], P(('groups', 'site', 'member')), parts along dimension 0, may hold values from 0.049804688 to 1
- w_gate: bfloat16 [16, 2880, 2880], P(('site', 'member')), may hold values from -0.109375 to 0.109375
- w_up: bfloat16 [16, 2880, 2880], P(('site', 'member')), may hold values from -0.109375 to 0.109375
- w_down: bfloat16 [16, 2880, 2880], P(('site', 'member')), may hold values from -0.109375 to 0.109375
Outputs:
- mixed: bfloat16 [2048, 2880], P(('groups', 'site', 'member')), parts along dimension 0
There are 2 independent parts, one for each index of `groups`. A program takes and returns all parts, laid end to end along the dimension named above; an argument that names none is the same for every part. Nothing has to cross between parts.
Inputs may be any that keep to these rules, and one draw needn't show every extreme that they name: `expert_ids`: each row names 4 different experts. At most 18 of the 64 tokens of one device name any one expert.
All inputs are finite; a program needn't handle non-finite values.
Results may differ from a plain program's by a relative error of at most 0.014.
Values may be sent and summed in bfloat16 or wider, within the bound.
A program may use at most 192 MiB of HBM per device.

v0:
```python
import jax
import jax.numpy as jnp
from jax import lax
from jax.sharding import PartitionSpec as P

EXP_SITE = 4


alpha_glu = 1.702


def weight_table(expert_ids, route_weights, experts):
    columns = lax.broadcasted_iota(jnp.int32, (1, 1, experts), 2)
    matches = expert_ids[:, :, None] == columns
    spread = jnp.where(matches, route_weights[:, :, None].astype(jnp.float32), 0.0)
    return jnp.sum(spread, axis=1).astype(jnp.bfloat16)


def pack_rows(inputs, needed, capacity):
    position = jnp.cumsum(needed.astype(jnp.int32), axis=0) - 1
    target = jnp.where(needed, position, capacity)
    group_ids = lax.broadcasted_iota(jnp.int32, needed.shape, 1)
    packed = jnp.zeros((needed.shape[1], capacity, inputs.shape[1]), inputs.dtype)
    spread_rows = jnp.broadcast_to(inputs[:, None, :], needed.shape + (inputs.shape[1],))
    packed = packed.at[group_ids, target].set(spread_rows, mode="drop")
    return (packed, jnp.minimum(target, capacity - 1), group_ids)


def expert_apply(received, gate_weight, up_weight, down_weight):
    feature_width = received.shape[-1]
    flat_rows = received.reshape(-1, feature_width)
    gate_value = jnp.dot(flat_rows, gate_weight, preferred_element_type=jnp.float32)
    up_value = jnp.dot(flat_rows, up_weight, preferred_element_type=jnp.float32)
    hidden = ((up_value + 1.0) * gate_value * jax.nn.sigmoid(alpha_glu * gate_value)).astype(
        jnp.bfloat16
    )
    produced = jnp.dot(hidden, down_weight, preferred_element_type=jnp.float32).astype(jnp.bfloat16)
    return produced.reshape(received.shape)


def body(tokens, expert_ids, route_weights, w_gate, w_up, w_down):
    site_count = lax.axis_size("site")
    members = lax.axis_size("member")
    experts = EXP_SITE * site_count
    split_count = members // EXP_SITE
    tok_count = tokens.shape[0]
    top_count = expert_ids.shape[1]
    mean_rows = tok_count * top_count // experts
    most_rows = mean_rows + max(1, mean_rows // 8)
    gate_weight = w_gate[0]
    up_weight = w_up[0]
    down_weight = w_down[0]
    route_table = weight_table(expert_ids, route_weights, experts)
    needed = route_table > 0
    packed, clipped, group_ids = pack_rows(tokens, needed, most_rows)
    outgoing = jnp.repeat(packed, split_count, axis=0)
    produced = expert_apply(
        lax.all_to_all(outgoing, ("site", "member"), split_axis=0, concat_axis=0, tiled=True),
        gate_weight,
        up_weight,
        down_weight,
    )
    returned = lax.all_to_all(produced, ("site", "member"), split_axis=0, concat_axis=0, tiled=True)
    per_expert = jnp.sum(
        returned.astype(jnp.float32).reshape(experts, split_count, most_rows, -1), axis=1
    )
    picked = per_expert[group_ids, clipped]
    weighted = route_table.astype(jnp.float32)[:, :, None] * picked
    site_terms = jnp.sum(weighted.reshape(tok_count, site_count, EXP_SITE, -1), axis=2)
    rounded = lax.optimization_barrier(site_terms.astype(jnp.bfloat16))
    mixed_out = jnp.sum(rounded.astype(jnp.float32), axis=1)
    return mixed_out.astype(jnp.bfloat16)


def solution(mesh):
    placed = (
        P(("groups", "site", "member"), None),
        P(("groups", "site", "member"), None),
        P(("groups", "site", "member"), None),
        P(("site", "member"), None, None),
        P(("site", "member"), None, None),
        P(("site", "member"), None, None),
    )
    return jax.shard_map(
        body,
        mesh=mesh,
        in_specs=placed,
        out_specs=P(("groups", "site", "member"), None),
        check_vma=False,
    )
```

profile of v0, /device:TPU:15, one launch (start us, length us, event | category | flops | bytes accessed | tf_op | source)
XLA Modules:
  0.0 233.0 jit_solution(5532169070408501611)
XLA Ops:
  0.0 0.7 convert_element_type.50
  0.7 0.7 select_reduce_fusion
  1.4 0.1 copy.37
  1.5 0.1 reduce_window_sum.11
  1.6 0.1 copy.40
  1.7 0.7 multiply_reduce_fusion.1
  2.4 0.1 copy.42
  2.5 0.7 and_reduce_fusion
  3.2 0.1 copy.41
  3.4 0.1 reshape.103
  3.4 4.0 %broadcast_in_dim.39 = bf16[64,16,2880]{2,1,0:T(8,128)(2,1)} broadcast(bf16[64,2880]{1,0:T(8,128)(2,1)} %param.6), dimensions={0,2} | broadcast | bytes 6266880 | tf_op jit(solution)/shard_map/broadcast_in_dim | solution.py:24
  7.4 10.3 %scatter_custom_fusion = bf16[288,2880]{1,0:T(8,128)(2,1)S(1)} fusion(s32[1024]{0:T(1024)S(1)} %reshape.103, bf16[1024,2880]{1,0:T(8,128)(2,1)} %bitcast.35, bf16[]{:T(256)} %constant.9.clone.1), kind=kCustom, calls=%fused_computation.15 | custom fusion | bytes 1659392
  17.7 0.3 copy.43
  18.0 57.2 %all_to_all.10 = bf16[16,18,2880]{2,1,0:T(8,128)(2,1)S(1)} all-to-all(bf16[16,18,2880]{2,1,0:T(8,128)(2,1)S(1)} %copy.43), channel_id=1, replica_groups=mesh['groups'=2,'site'=4,'member'=4] {'site','member'}, dimensions={0} | all-to-all | bytes 3317760 | tf_op jit(solution)/shard_map/all_to_all | solution.py:58
  75.2 1.8 reshape.90
  77.0 0.0 copy-start
  77.0 0.0 slice-start
  77.0 0.0 slice-start.1
  77.0 0.0 slice-start.2
  77.0 10.0 %fusion.2 = f32[288,2880]{1,0:T(8,128)S(1)} fusion(bf16[288,2880]{1,0:T(8,128)(2,1)} %reshape.90, bf16[1,2880,2880]{2,1,0:T(8,128)(2,1)} %param.9), kind=kOutput, calls=%fused_computation.4 | convolution fusion | flops 4777574400 | bytes 21565440 | tf_op jit(solution)/shard_map/dot_general | solution.py:32
  87.0 0.0 copy-done
  87.0 0.0 slice-start.3
  87.1 0.0 slice-start.4
  87.1 9.7 %fusion.15 = bf16[288,2880]{1,0:T(8,128)(2,1)S(1)} fusion(f32[288,2880]{1,0:T(8,128)S(1)} %fusion.2, bf16[288,2880]{1,0:T(8,128)(2,1)S(1)} %copy-done, bf16[1,2880,2880]{2,1,0:T(8,128)(2,1)} %param.10), kind=kOutput, calls=%fused_computation.12 | convolution fusion | flops 4784209920 | bytes 23224320 | tf_op jit(solution)/shard_map/dot_general | solution.py:33
  96.8 0.0 slice-done
  96.8 0.0 slice-done.1
  96.8 0.0 slice-done.2
  96.8 0.0 slice-done.3
  96.8 0.0 slice-done.4
  96.9 5.6 %fusion.18 = bf16[288,2880]{1,0:T(8,128)(2,1)S(1)} fusion(bf16[288,2880]{1,0:T(8,128)(2,1)S(1)} %fusion.15, bf16[1,2880,2880]{2,1,0:T(8,128)(2,1)S(1)} %bitcast.38), kind=kOutput, calls=%fused_computation.13 | convolution fusion | flops 4778403840 | bytes 19906560 | tf_op jit(solution)/shard_map/dot_general | solution.py:37
  102.5 1.7 reshape.91
  104.2 5.8 %all-to-all-start.1 = ((bf16[16,18,2880]{2,1,0:T(8,128)(2,1)}), bf16[16,18,2880]{2,1,0:T(8,128)(2,1)}, u32[]{:S(2)}, u32[]{:S(2)}) async-start(bf16[16,18,2880]{2,1,0:T(8,128)(2,1)} %reshape.91), calls=%async_computation.1 | async-start | bytes 4521984 | tf_op jit(solution)/shard_map/all_to_all | solution.py:63
  110.0 0.1 copy.38
  110.1 0.1 reshape.97
  110.1 0.1 copy.39
  110.3 50.8 %all-to-all-done.1 = bf16[16,18,2880]{2,1,0:T(8,128)(2,1)} async-done(((bf16[16,18,2880]{2,1,0:T(8,128)(2,1)}), bf16[16,18,2880]{2,1,0:T(8,128)(2,1)}, u32[]{:S(2)}, u32[]{:S(2)}) %all-to-all-start.1) | async-done | bytes 1658912 | tf_op jit(solution)/shard_map/all_to_all | solution.py:63
  161.0 1.9 copy_convert_fusion
  162.9 22.7 %gather_fusion = f32[1024,2880]{1,0:T(8,128)} fusion(f32[16,18,2880]{2,0,1:T(8,128)S(1)} %copy_convert_fusion, s32[1024]{0:T(1024)S(1)} %reshape.97), kind=kCustom, calls=%fused_computation | custom fusion | bytes 23601152 | tf_op jit(solution)/shard_map/gather | solution.py:67
  185.6 14.2 %gather.6 = f32[64,4,4,2880]{3,2,1,0:T(4,128)} reshape(f32[1024,2880]{1,0:T(8,128)} %gather_fusion) | data formatting | bytes 23592960 | tf_op jit(solution)/shard_map/gather | solution.py:67
  199.8 30.4 %multiply_reduce_fusion = bf16[64,4,2880]{2,1,0:T(4,128)(2,1)S(1)} fusion(f32[64,4,4,2880]{3,2,1,0:T(4,128)} %gather.6, f32[64,4,4]{2,1,0:T(4,128)S(1)} %copy.39), kind=kLoop, calls=%fused_computation.8 | loop fusion | flops 5160960 | bytes 13275136 | tf_op jit(solution)/shard_map/reduce_sum | solution.py:69
  230.2 2.8 %reduce_sum.36 = bf16[64,2880]{1,0:T(8,128)(2,1)} reduce(bf16[64,4,2880]{2,1,0:T(4,128)(2,1)S(1)} %multiply_reduce_fusion, bf16[]{:T(256)} %constant.9.clone.1), dimensions={1}, to_apply=%region_4.5 | reduce | flops 552960 | bytes 1843202 | tf_op jit(solution)/shard_map/reduce_sum | solution.py:71
  (5 shorter events, 0.1 us)
Async XLA Ops:
  77.0 10.0 %copy-start = (bf16[288,2880]{1,0:T(8,128)(2,1)S(1)}, bf16[288,2880]{1,0:T(8,128)(2,1)}, u32[]{:S(2)}) copy-start(bf16[288,2880]{1,0:T(8,128)(2,1)} %reshape.90) | copy-start | bytes 4976644
  77.0 19.8 %slice-start = ((s8[16957440]{0:T(1024)(128)(4,1)}), s8[4194304]{0:T(1024)(128)(4,1)S(1)}, s32[]{:S(2)}) async-start(s8[16957440]{0:T(1024)(128)(4,1)} %bitcast.37), calls=%async_computation.2 | async-start | bytes 8388608
  77.0 19.8 %slice-start.1 = ((s8[16957440]{0:T(1024)(128)(4,1)}), s8[4194304]{0:T(1024)(128)(4,1)S(1)}, s32[]{:S(2)}) async-start(s8[16957440]{0:T(1024)(128)(4,1)} %bitcast.37), calls=%async_computation.3 | async-start | bytes 8388608
  77.0 19.8 %slice-start.2 = ((s8[16957440]{0:T(1024)(128)(4,1)}), s8[4194304]{0:T(1024)(128)(4,1)S(1)}, s32[]{:S(2)}) async-start(s8[16957440]{0:T(1024)(128)(4,1)} %bitcast.37), calls=%async_computation.4 | async-start | bytes 8388608
  87.0 9.8 %slice-start.3 = ((s8[16957440]{0:T(1024)(128)(4,1)}), s8[4194304]{0:T(1024)(128)(4,1)S(1)}, s32[]{:S(2)}) async-start(s8[16957440]{0:T(1024)(128)(4,1)} %bitcast.37), calls=%async_computation.5 | async-start | bytes 8388608
  87.1 9.8 %slice-start.4 = ((s8[16957440]{0:T(1024)(128)(4,1)}), s8[180224]{0:T(1024)(128)(4,1)S(1)}, s32[]{:S(2)}) async-start(s8[16957440]{0:T(1024)(128)(4,1)} %bitcast.37), calls=%async_computation.6 | async-start | bytes 360448
  104.2 56.9 %all-to-all-start.1 = ((bf16[16,18,2880]{2,1,0:T(8,128)(2,1)}), bf16[16,18,2880]{2,1,0:T(8,128)(2,1)}, u32[]{:S(2)}, u32[]{:S(2)}) async-start(bf16[16,18,2880]{2,1,0:T(8,128)(2,1)} %reshape.91), calls=%async_computation.1 | async-start | bytes 4521984 | tf_op jit(solution)/shard_map/all_to_all | solution.py:63
where the time goes:
time: 234 us; the launch traced here: 233 us
  blocking collectives  57.2 us (24%)
  local copies, waits for them, and re-layouts  55.7 us (24%)
  waiting for transfers between devices  50.8 us (22%)
  other arithmetic  38 us (16%)
  matrix products  25.3 us (11%)
  starting transfers between devices  5.82 us (2%)
    all_to_all x1, blocking collectives, body(): lax.all_to_all(outgoing, ('site', 'member'), split_axis=0, concat_axis=0,...  57.2 us
    all_to_all x1, waiting for transfers between devices, body(): lax.all_to_all(produced, ('site', 'member'), split_axis=0, concat_axis=0,...  50.8 us
    gather x2, local copies, waits for them, and re-layouts, body(): picked = per_expert[group_ids, clipped]  36.9 us
    reduce_sum x1, other arithmetic, body(): jnp.sum(weighted.reshape(tok_count, site_count, EXP_SITE, -1), axis=2)  30.4 us
    unnamed x16, local copies, waits for them, and re-layouts  10.6 us
    dot_general x1, matrix products, expert_apply(): jnp.dot(flat_rows, gate_weight, preferred_element_type=jnp.float32)  10 us
    dot_general x1, matrix products, expert_apply(): up_value = jnp.dot(flat_rows, up_weight, preferred_element_type=jnp.float32)  9.73 us
    all_to_all x1, starting transfers between devices, body(): lax.all_to_all(produced, ('site', 'member'), split_axis=0, concat_axis=0,...  5.82 us
  transfers between devices with their start and end apart: 1, of which 1 were waited for; matrix products, arithmetic and copies ran while one was open for 0% of the time, Pallas kernels for 0%

commit v1 on v0

v1 whole, which is shorter than its diff:
```python
import jax
import jax.numpy as jnp
from jax import lax
from jax.sharding import PartitionSpec as P

EXP_SITE = 4
ALPHA = 1.702
AXES = ("site", "member")


def routing(expert_ids, route_weights, experts, most):
    count = expert_ids.shape[0]
    columns = lax.broadcasted_iota(jnp.int32, (1, 1, experts), 2)
    matches = expert_ids[:, :, None] == columns
    hit = jnp.any(matches, axis=1)
    table = jnp.sum(jnp.where(matches, route_weights[:, :, None].astype(jnp.float32), 0.0), axis=1)
    row = lax.broadcasted_iota(jnp.int32, (count, count), 0)
    col = lax.broadcasted_iota(jnp.int32, (count, count), 1)
    before = (col < row).astype(jnp.bfloat16)
    position = lax.dot_general(
        hit.astype(jnp.bfloat16), before, (((0,), (1,)), ((), ())), preferred_element_type=jnp.float32
    ).astype(jnp.int32)
    slot = lax.broadcasted_iota(jnp.int32, (experts, most, count), 1)
    chosen = (position[:, None, :] == slot) & hit.T[:, None, :]
    select = chosen.astype(jnp.bfloat16)
    weights = jnp.where(chosen, table.T[:, None, :], 0.0).astype(jnp.bfloat16)
    return select, weights


def expert_apply(rows, gate_weight, up_weight, down_weight):
    gate = jnp.dot(rows, gate_weight, preferred_element_type=jnp.float32)
    up = jnp.dot(rows, up_weight, preferred_element_type=jnp.float32)
    hidden = ((up + 1.0) * gate * jax.nn.sigmoid(ALPHA * gate)).astype(jnp.bfloat16)
    return jnp.dot(hidden, down_weight, preferred_element_type=jnp.float32).astype(jnp.bfloat16)


def body(tokens, expert_ids, route_weights, w_gate, w_up, w_down):
    experts = EXP_SITE * lax.axis_size("site")
    split = lax.axis_size("member") // EXP_SITE
    count, width = tokens.shape
    mean_rows = count * expert_ids.shape[1] // experts
    most = mean_rows + max(1, mean_rows // 8)
    select, weights = routing(expert_ids, route_weights, experts, most)
    packed = jnp.dot(select.reshape(experts * most, count), tokens, preferred_element_type=jnp.float32)
    packed = packed.astype(jnp.bfloat16).reshape(experts, most, width)
    outgoing = jnp.repeat(packed, split, axis=0)
    received = lax.all_to_all(outgoing, AXES, split_axis=0, concat_axis=0, tiled=True)
    produced = expert_apply(received.reshape(-1, width), w_gate[0], w_up[0], w_down[0])
    returned = lax.all_to_all(produced.reshape(received.shape), AXES, split_axis=0, concat_axis=0, tiled=True)
    spread = jnp.repeat(weights, split, axis=0).reshape(experts * split * most, count)
    mixed = lax.dot_general(
        spread, returned.reshape(-1, width), (((0,), (0,)), ((), ())), preferred_element_type=jnp.float32
    )
    return mixed.astype(jnp.bfloat16)


def solution(mesh):
    rows = P(("groups", "site", "member"), None)
    held = P(("site", "member"), None, None)
    return jax.shard_map(
        body,
        mesh=mesh,
        in_specs=(rows, rows, rows, held, held, held),
        out_specs=rows,
        check_vma=False,
    )
```

time: 234 us -> 149 us (0.64)
  local copies, waits for them, and re-layouts: 55.7 us -> 5.87 us
  other arithmetic: 38 us -> 0.76 us
  matrix products: 25.3 us -> 28.5 us
    gather x2 -> x0, local copies, waits for them, and re-layouts: 36.9 us -> none  [body(): picked = per_expert[group_ids, clipped]]
    reduce_sum x3 -> x1, other arithmetic: 33.9 us -> 0.01 us  [routing(): jnp.sum(jnp.where(matches, route_weights[:, :, None].astype(jnp.float32),...]
    unnamed x16 -> x18, local copies, waits for them, and re-layouts: 10.6 us -> 0.05 us
    broadcast_in_dim x1 -> x0, local copies, waits for them, and re-layouts: 3.97 us -> none  [pack_rows(): jnp.broadcast_to(inputs[:, None, :], needed.shape + (inputs.shape[1],))]
    dot_general x2 -> x5, matrix products: 19.7 us -> 22.9 us  [the longest x1 9.95 us: expert_apply(): up = jnp.dot(rows, up_weight, preferred_element_type=jnp.float32)]
    convert_element_type x3 -> x1, other arithmetic: 2.55 us -> 0.01 us  [routing(): route_weights[:, :, None].astype(jnp.float32)]
where the time goes in v1:
time: 149 us
  blocking collectives  57.3 us (38%)
  waiting for transfers between devices  50.9 us (34%)
  matrix products  28.5 us (19%)
  local copies, waits for them, and re-layouts  5.87 us (4%)
  starting transfers between devices  5.16 us (3%)
    all_to_all x1, blocking collectives, body(): lax.all_to_all(outgoing, AXES, split_axis=0, concat_axis=0, tiled=True)  57.3 us
    all_to_all x1, waiting for transfers between devices, body(): lax.all_to_all(produced.reshape(received.shape), AXES, split_axis=0, conc...  50.9 us
    dot_general x1, matrix products, expert_apply(): up = jnp.dot(rows, up_weight, preferred_element_type=jnp.float32)  9.95 us
    dot_general x1, matrix products, expert_apply(): gate = jnp.dot(rows, gate_weight, preferred_element_type=jnp.float32)  9.71 us
    dot_general x1, matrix products, expert_apply(): jnp.dot(hidden, down_weight, preferred_element_type=jnp.float32)  5.6 us
    all_to_all x1, starting transfers between devices, body(): lax.all_to_all(produced.reshape(received.shape), AXES, split_axis=0, conc...  5.16 us
  transfers between devices with their start and end apart: 1, of which 1 were waited for; matrix products, arithmetic and copies ran while one was open for 0% of the time, Pallas kernels for 0%

profile of v1, /device:TPU:15, one launch (start us, length us, event | category | flops | bytes accessed | tf_op | source)
XLA Modules:
  0.0 148.7 jit_solution(1448879458360436247)
XLA Ops:
  0.0 0.0 copy-start
  0.0 0.7 fusion.30
  0.7 0.1 convolution_convert_fusion.1
  1.0 0.1 iota.32
  1.1 0.0 copy-done
  1.1 1.9 %convolution_convert_fusion = bf16[288,2880]{1,0:T(8,128)(2,1)} fusion(bf16[64,2880]{1,0:T(8,128)(2,1)S(1)} %copy-done, pred[288,64]{1,0:T(32,128)(4,1)S(1)} %and.15, s32[288,64]{1,0:T(8,128)S(1)} %eq.31, s32[288]{0:T(512)S(1)} %iota.32), kind=kOutput, calls=%fused_computation.11 | convolution fusion | flops 107034624 | bytes 2120832 | tf_op jit(solution)/shard_map/dot_general | solution.py:44
  3.0 1.8 %reshape_broadcast_in_dim_reshape.3 = bf16[16,18,2880]{2,1,0:T(8,128)(2,1)S(1)} reshape(bf16[288,2880]{1,0:T(8,128)(2,1)} %convolution_convert_fusion) | data formatting | bytes 3317760 | tf_op jit(solution)/shard_map/reshape;broadcast_in_dim;reshape | solution.py:46
  4.7 57.3 %all_to_all.10 = bf16[16,18,2880]{2,1,0:T(8,128)(2,1)} all-to-all(bf16[16,18,2880]{2,1,0:T(8,128)(2,1)S(1)} %reshape_broadcast_in_dim_reshape.3), channel_id=1, replica_groups=mesh['groups'=2,'site'=4,'member'=4] {'site','member'}, dimensions={0} | all-to-all | bytes 3317760 | tf_op jit(solution)/shard_map/all_to_all | solution.py:47
  62.0 2.2 %reshape.17 = bf16[288,2880]{1,0:T(8,128)(2,1)S(1)} reshape(bf16[16,18,2880]{2,1,0:T(8,128)(2,1)} %all_to_all.10) | data formatting | bytes 3317760 | tf_op jit(solution)/shard_map/reshape | solution.py:48
  64.2 0.0 slice-start
  64.2 0.0 slice-start.1
  64.2 0.0 slice-start.2
  64.2 9.7 %fusion.2 = f32[288,2880]{1,0:T(8,128)S(1)} fusion(bf16[288,2880]{1,0:T(8,128)(2,1)S(1)} %reshape.17, bf16[1,2880,2880]{2,1,0:T(8,128)(2,1)} %param.9), kind=kOutput, calls=%fused_computation.2 | convolution fusion | flops 4777574400 | bytes 21565440 | tf_op jit(solution)/shard_map/dot_general | solution.py:31
  73.9 0.0 slice-start.3
  74.0 0.0 slice-start.4
  74.0 9.9 %fusion.15 = bf16[288,2880]{1,0:T(8,128)(2,1)S(1)} fusion(f32[288,2880]{1,0:T(8,128)S(1)} %fusion.2, bf16[288,2880]{1,0:T(8,128)(2,1)S(1)} %reshape.17, bf16[1,2880,2880]{2,1,0:T(8,128)(2,1)} %param.10), kind=kOutput, calls=%fused_computation.9 | convolution fusion | flops 4784209920 | bytes 23224320 | tf_op jit(solution)/shard_map/dot_general | solution.py:32
  83.9 0.0 slice-done
  83.9 0.0 slice-done.1
  83.9 0.0 slice-done.2
  84.0 0.0 slice-done.3
  84.0 0.0 slice-done.4
  84.0 5.6 %fusion.18 = bf16[288,2880]{1,0:T(8,128)(2,1)S(1)} fusion(bf16[288,2880]{1,0:T(8,128)(2,1)S(1)} %fusion.15, bf16[1,2880,2880]{2,1,0:T(8,128)(2,1)S(1)} %bitcast.35), kind=kOutput, calls=%fused_computation.10 | convolution fusion | flops 4778403840 | bytes 19906560 | tf_op jit(solution)/shard_map/dot_general | solution.py:34
  89.6 0.0 copy-start.3
  89.6 0.0 copy-start.2
  89.6 0.0 copy-start.1
  89.6 1.7 %reshape.18 = bf16[16,18,2880]{2,1,0:T(8,128)(2,1)} reshape(bf16[288,2880]{1,0:T(8,128)(2,1)S(1)} %fusion.18) | data formatting | bytes 3317760 | tf_op jit(solution)/shard_map/reshape | solution.py:49
  91.3 5.2 %all-to-all-start.1 = ((bf16[16,18,2880]{2,1,0:T(8,128)(2,1)}), bf16[16,18,2880]{2,1,0:T(8,128)(2,1)S(1)}, u32[]{:S(2)}, u32[]{:S(2)}) async-start(bf16[16,18,2880]{2,1,0:T(8,128)(2,1)} %reshape.18), calls=%async_computation.1 | async-start | bytes 4521984 | tf_op jit(solution)/shard_map/all_to_all | solution.py:49
  96.5 0.0 copy-done.3
  96.5 0.0 copy-done.2
  96.5 50.9 %all-to-all-done.1 = bf16[16,18,2880]{2,1,0:T(8,128)(2,1)S(1)} async-done(((bf16[16,18,2880]{2,1,0:T(8,128)(2,1)}), bf16[16,18,2880]{2,1,0:T(8,128)(2,1)S(1)}, u32[]{:S(2)}, u32[]{:S(2)}) %all-to-all-start.1) | async-done | bytes 1658912 | tf_op jit(solution)/shard_map/all_to_all | solution.py:49
  147.4 1.3 fusion.21
  148.7 0.0 copy-done.1
  (8 shorter events, 0.1 us)
Async XLA Ops:
  0.0 1.1 copy-start
  64.2 19.7 %slice-start = ((s8[16957440]{0:T(1024)(128)(4,1)}), s8[4194304]{0:T(1024)(128)(4,1)S(1)}, s32[]{:S(2)}) async-start(s8[16957440]{0:T(1024)(128)(4,1)} %bitcast.34), calls=%async_computation.2 | async-start | bytes 8388608
  64.2 19.7 %slice-start.1 = ((s8[16957440]{0:T(1024)(128)(4,1)}), s8[4194304]{0:T(1024)(128)(4,1)S(1)}, s32[]{:S(2)}) async-start(s8[16957440]{0:T(1024)(128)(4,1)} %bitcast.34), calls=%async_computation.3 | async-start | bytes 8388608
  64.2 19.7 %slice-start.2 = ((s8[16957440]{0:T(1024)(128)(4,1)}), s8[4194304]{0:T(1024)(128)(4,1)S(1)}, s32[]{:S(2)}) async-start(s8[16957440]{0:T(1024)(128)(4,1)} %bitcast.34), calls=%async_computation.4 | async-start | bytes 8388608
  73.9 10.0 %slice-start.3 = ((s8[16957440]{0:T(1024)(128)(4,1)}), s8[4194304]{0:T(1024)(128)(4,1)S(1)}, s32[]{:S(2)}) async-start(s8[16957440]{0:T(1024)(128)(4,1)} %bitcast.34), calls=%async_computation.5 | async-start | bytes 8388608
  74.0 10.0 %slice-start.4 = ((s8[16957440]{0:T(1024)(128)(4,1)}), s8[180224]{0:T(1024)(128)(4,1)S(1)}, s32[]{:S(2)}) async-start(s8[16957440]{0:T(1024)(128)(4,1)} %bitcast.34), calls=%async_computation.6 | async-start | bytes 360448
  89.6 6.9 %copy-start.3 = (bf16[64,4]{0,1:T(4,128)(2,1)S(1)}, bf16[64,4]{0,1:T(4,128)(2,1)}, u32[]{:S(2)}) copy-start(bf16[64,4]{0,1:T(4,128)(2,1)} %param.8) | copy-start | bytes 1540
  89.6 6.9 %copy-start.2 = (s32[64,4]{0,1:T(4,128)S(1)}, s32[64,4]{0,1:T(4,128)}, u32[]{:S(2)}) copy-start(s32[64,4]{0,1:T(4,128)} %param.7) | copy-start | bytes 3076
  89.6 59.1 %copy-start.1 = (bf16[64,2880]{1,0:T(8,128)(2,1)S(1)}, bf16[64,2880]{1,0:T(8,128)(2,1)}, u32[]{:S(2)}) copy-start(bf16[64,2880]{1,0:T(8,128)(2,1)} %param.6) | copy-start | bytes 1105924
  91.3 56.1 %all-to-all-start.1 = ((bf16[16,18,2880]{2,1,0:T(8,128)(2,1)}), bf16[16,18,2880]{2,1,0:T(8,128)(2,1)S(1)}, u32[]{:S(2)}, u32[]{:S(2)}) async-start(bf16[16,18,2880]{2,1,0:T(8,128)(2,1)} %reshape.18), calls=%async_computation.1 | async-start | bytes 4521984 | tf_op jit(solution)/shard_map/all_to_all | solution.py:49

commit v2 on v1

--- a/solution.py
+++ b/solution.py
@@ -6,6 +6,7 @@
 EXP_SITE = 4
 ALPHA = 1.702
 AXES = ("site", "member")
+ROWS, LANES = 16, 128
 
 
 def routing(expert_ids, route_weights, experts, most):
@@ -34,22 +35,56 @@
     return jnp.dot(hidden, down_weight, preferred_element_type=jnp.float32).astype(jnp.bfloat16)
 
 
+def fold_plan(most, width):
+    extra = most % ROWS
+    if most > ROWS and extra and ROWS % extra == 0 and most // ROWS == 1:
+        pieces = ROWS // extra
+        return ROWS, pieces, LANES * (-(-width // (pieces * LANES)))
+    return -(-most // ROWS) * ROWS, 0, 0
+
+
+def fold(rows, blocks, kept, pieces, piece, width):
+    main = rows[: blocks * kept]
+    if not pieces:
+        return main.reshape(blocks, kept, width)
+    further = rows[blocks * kept :]
+    main = jnp.pad(main, ((0, 0), (0, -width % LANES)))
+    further = jnp.pad(further, ((0, 0), (0, pieces * piece - width))).reshape(blocks * kept, piece)
+    return jnp.concatenate([main, further], axis=1).reshape(blocks, kept, -1)
+
+
+def unfold(blocks_in, blocks, kept, pieces, piece, width):
+    flat = blocks_in.reshape(blocks * kept, -1)
+    if not pieces:
+        return flat
+    main = flat[:, :width]
+    further = flat[:, width + -width % LANES :].reshape(-1, pieces * piece)[:, :width]
+    return jnp.concatenate([main, further], axis=0)
+
+
 def body(tokens, expert_ids, route_weights, w_gate, w_up, w_down):
     experts = EXP_SITE * lax.axis_size("site")
     split = lax.axis_size("member") // EXP_SITE
     count, width = tokens.shape
     mean_rows = count * expert_ids.shape[1] // experts
     most = mean_rows + max(1, mean_rows // 8)
-    select, weights = routing(expert_ids, route_weights, experts, most)
-    packed = jnp.dot(select.reshape(experts * most, count), tokens, preferred_element_type=jnp.float32)
-    packed = packed.astype(jnp.bfloat16).reshape(experts, most, width)
-    outgoing = jnp.repeat(packed, split, axis=0)
-    received = lax.all_to_all(outgoing, AXES, split_axis=0, concat_axis=0, tiled=True)
-    produced = expert_apply(received.reshape(-1, width), w_gate[0], w_up[0], w_down[0])
-    returned = lax.all_to_all(produced.reshape(received.shape), AXES, split_axis=0, concat_axis=0, tiled=True)
-    spread = jnp.repeat(weights, split, axis=0).reshape(experts * split * most, count)
+    blocks = experts * split
+    kept, pieces, piece = fold_plan(most, width)
+    plan = (blocks, kept, pieces, piece, width)
+    total = most if pieces else kept
+
+    def ordered(table):
+        table = jnp.repeat(table, split, axis=0)
+        parts = [table[:, :kept], table[:, kept:]] if pieces else [table]
+        return jnp.concatenate([p.reshape(-1, count) for p in parts], axis=0)
+
+    select, weights = routing(expert_ids, route_weights, experts, total)
+    packed = jnp.dot(ordered(select), tokens, preferred_element_type=jnp.float32).astype(jnp.bfloat16)
+    received = lax.all_to_all(fold(packed, *plan), AXES, split_axis=0, concat_axis=0, tiled=True)
+    produced = expert_apply(unfold(received, *plan), w_gate[0], w_up[0], w_down[0])
+    returned = lax.all_to_all(fold(produced, *plan), AXES, split_axis=0, concat_axis=0, tiled=True)
     mixed = lax.dot_general(
-        spread, returned.reshape(-1, width), (((0,), (0,)), ((), ())), preferred_element_type=jnp.float32
+        ordered(weights), unfold(returned, *plan), (((0,), (0,)), ((), ())), preferred_element_type=jnp.float32
     )
     return mixed.astype(jnp.bfloat16)
 

time: 149 us -> 133 us (0.89)
  blocking collectives: 57.3 us -> 45.2 us
  waiting for transfers between devices: 50.9 us -> 38.9 us
  matrix products: 28.5 us -> 37.7 us
  local copies, waits for them, and re-layouts: 5.87 us -> 3.35 us
  other arithmetic: 0.76 us -> 2.28 us
    dot_general x1, matrix products: 5.6 us -> 23.1 us  [expert_apply(): jnp.dot(hidden, down_weight, preferred_element_type=jnp.float32)]
    all_to_all x1, blocking collectives: 57.3 us -> 45.2 us  [body(): lax.all_to_all(fold(packed, *plan), AXES, split_axis=0, concat_axis=0, ti...]
    all_to_all x1, waiting for transfers between devices: 50.9 us -> 38.9 us  [body(): lax.all_to_all(fold(produced, *plan), AXES, split_axis=0, concat_axis=0,...]
    dot_general x3 -> x2, matrix products: 13.1 us -> 3.21 us  [the longest x1 2.63 us: body(): lax.dot_general(ordered(weights), unfold(returned, *plan), (((0,), (0,)),...]
    reshape x2, local copies, waits for them, and re-layouts: 3.87 us -> 0.19 us  [unfold(): flat[:, width + -width % LANES:].reshape(-1, pieces * piece)[:, :width]]
    another operation x1 -> x0, local copies, waits for them, and re-layouts: 1.77 us -> none  [body(): outgoing = jnp.repeat(packed, split, axis=0)]
    slice x0 -> x14, local copies, waits for them, and re-layouts: none -> 1.69 us  [the longest x2 1.35 us: unfold(): main = flat[:, :width]]
where the time goes in v2:
time: 133 us
  blocking collectives  45.2 us (34%)
  waiting for transfers between devices  38.9 us (29%)
  matrix products  37.7 us (28%)
  starting transfers between devices  5.48 us (4%)
  local copies, waits for them, and re-layouts  3.35 us (3%)
  other arithmetic  2.28 us (2%)
    all_to_all x1, blocking collectives, body(): lax.all_to_all(fold(packed, *plan), AXES, split_axis=0, concat_axis=0, ti...  45.2 us
    all_to_all x1, waiting for transfers between devices, body(): lax.all_to_all(fold(produced, *plan), AXES, split_axis=0, concat_axis=0,...  38.9 us
    dot_general x1, matrix products, expert_apply(): jnp.dot(hidden, down_weight, preferred_element_type=jnp.float32)  23.1 us
    dot_general x1, matrix products, expert_apply(): gate = jnp.dot(rows, gate_weight, preferred_element_type=jnp.float32)  11.2 us
    all_to_all x1, starting transfers between devices, body(): lax.all_to_all(fold(produced, *plan), AXES, split_axis=0, concat_axis=0,...  5.48 us
  transfers between devices with their start and end apart: 1, of which 1 were waited for; matrix products, arithmetic and copies ran while one was open for 0% of the time, Pallas kernels for 0%

profile of v2, /device:TPU:15, one launch (start us, length us, event | category | flops | bytes accessed | tf_op | source)
XLA Modules:
  0.0 133.1 jit_solution(16250525168091522183)
XLA Ops:
  0.0 0.0 copy-start
  0.0 0.7 fusion.34
  0.7 0.1 convolution_convert_fusion.2
  1.0 0.0 copy-done
  1.0 0.6 convolution_convert_fusion
  1.6 0.1 slice.60
  1.7 0.1 pad.14
  1.9 0.1 concatenate.31
  2.0 0.1 pad_maximum_fusion
  2.1 45.2 %all_to_all.10 = bf16[16,16,3328]{2,1,0:T(8,128)(2,1)S(1)} all-to-all(bf16[16,16,3328]{2,1,0:T(8,128)(2,1)S(1)} %pad_maximum_fusion), channel_id=1, replica_groups=mesh['groups'=2,'site'=4,'member'=4] {'site','member'}, dimensions={0} | all-to-all | bytes 3407872 | tf_op jit(solution)/shard_map/all_to_all | solution.py:83
  47.3 0.1 slice.62
  47.4 0.0 copy-start.2
  47.5 0.1 reshape.45
  47.6 1.0 copy-done.2
  48.6 11.2 %fusion.2 = f32[288,2880]{1,0:T(8,128)} fusion(bf16[1,2880,2880]{2,1,0:T(8,128)(2,1)} %param.9, bf16[32,2880]{1,0:T(8,128)(2,1)S(1)} %slice.64, bf16[256,2880]{1,0:T(8,128)(2,1)S(1)} %slice.62), kind=kOutput, calls=%fused_computation.2 | convolution fusion | flops 4780892160 | bytes 21565440 | tf_op jit(solution)/shard_map/dot_general | solution.py:32
  59.7 23.1 %fusion.18 = bf16[288,2880]{1,0:T(8,128)(2,1)S(1)} fusion(bf16[1,2880,2880]{2,1,0:T(8,128)(2,1)} %param.11, f32[288,2880]{1,0:T(8,128)} %fusion.2, bf16[1,2880,2880]{2,1,0:T(8,128)(2,1)} %param.10, bf16[32,2880]{1,0:T(8,128)(2,1)S(1)} %slice.64, bf16[256,2880]{1,0:T(8,128)(2,1)} %copy-done.2), kind=kOutput, calls=%fused_computation.10 | convolution fusion | flops 9565931520 | bytes 39813120 | tf_op jit(solution)/shard_map/dot_general | solution.py:35
  82.9 0.1 slice.65
  83.0 0.1 pad.16
  83.2 0.1 concatenate.35
  83.3 0.0 copy-start.4
  83.3 0.0 copy-start.3
  83.3 1.3 pad_maximum_fusion.1
  84.6 5.5 %all-to-all-start.1 = ((bf16[16,16,3328]{2,1,0:T(8,128)(2,1)}), bf16[16,16,3328]{2,1,0:T(8,128)(2,1)S(1)}, u32[]{:S(2)}, u32[]{:S(2)}) async-start(bf16[16,16,3328]{2,1,0:T(8,128)(2,1)} %pad_maximum_fusion.1), calls=%async_computation.1 | async-start | bytes 3407872 | tf_op jit(solution)/shard_map/all_to_all | solution.py:85
  90.1 0.0 copy-done.4
  90.1 0.0 copy-done.3
  90.1 0.0 copy-start.1
  90.2 38.9 %all-to-all-done.1 = bf16[16,16,3328]{2,1,0:T(8,128)(2,1)S(1)} async-done(((bf16[16,16,3328]{2,1,0:T(8,128)(2,1)}), bf16[16,16,3328]{2,1,0:T(8,128)(2,1)S(1)}, u32[]{:S(2)}, u32[]{:S(2)}) %all-to-all-start.1) | async-done | bytes 1703968 | tf_op jit(solution)/shard_map/all_to_all | solution.py:85
  129.1 1.2 slice.67
  130.4 0.1 reshape.47
  130.5 2.6 %convolution_convert_fusion.1 = bf16[64,2880]{1,0:T(8,128)(2,1)} fusion(bf16[32,2880]{1,0:T(8,128)(2,1)S(1)} %slice.69, bf16[256,2880]{1,0:T(8,128)(2,1)} %slice.67, bf16[32,64]{1,0:T(8,128)(2,1)S(1)} %bitcast.45, bf16[256,64]{1,0:T(8,128)(2,1)S(1)} %bitcast.40), kind=kOutput, calls=%fused_computation.12 | convolution fusion | flops 109744128 | bytes 2064384 | tf_op jit(solution)/shard_map/dot_general | solution.py:86
  133.1 0.0 copy-done.1
  (16 shorter events, 0.3 us)
Async XLA Ops:
  0.0 1.0 copy-start
  47.4 1.1 copy-start.2
  83.3 6.8 %copy-start.4 = (bf16[64,4]{0,1:T(4,128)(2,1)S(1)}, bf16[64,4]{0,1:T(4,128)(2,1)}, u32[]{:S(2)}) copy-start(bf16[64,4]{0,1:T(4,128)(2,1)} %param.8) | copy-start | bytes 1540
  83.3 6.8 %copy-start.3 = (s32[64,4]{0,1:T(4,128)S(1)}, s32[64,4]{0,1:T(4,128)}, u32[]{:S(2)}) copy-start(s32[64,4]{0,1:T(4,128)} %param.7) | copy-start | bytes 3076
  84.6 44.5 %all-to-all-start.1 = ((bf16[16,16,3328]{2,1,0:T(8,128)(2,1)}), bf16[16,16,3328]{2,1,0:T(8,128)(2,1)S(1)}, u32[]{:S(2)}, u32[]{:S(2)}) async-start(bf16[16,16,3328]{2,1,0:T(8,128)(2,1)} %pad_maximum_fusion.1), calls=%async_computation.1 | async-start | bytes 3407872 | tf_op jit(solution)/shard_map/all_to_all | solution.py:85
  90.1 43.0 %copy-start.1 = (bf16[64,2880]{1,0:T(8,128)(2,1)S(1)}, bf16[64,2880]{1,0:T(8,128)(2,1)}, u32[]{:S(2)}) copy-start(bf16[64,2880]{1,0:T(8,128)(2,1)} %param.6) | copy-start | bytes 1105924

commit v3 on v2

--- a/solution.py
+++ b/solution.py
@@ -1,12 +1,17 @@
+import functools
+
 import jax
 import jax.numpy as jnp
 from jax import lax
+from jax.experimental import pallas as pl
+from jax.experimental.pallas import tpu as pltpu
 from jax.sharding import PartitionSpec as P
 
 EXP_SITE = 4
 ALPHA = 1.702
 AXES = ("site", "member")
 ROWS, LANES = 16, 128
+CHUNK = 512
 
 
 def routing(expert_ids, route_weights, experts, most):
@@ -28,11 +33,54 @@
     return select, weights
 
 
-def expert_apply(rows, gate_weight, up_weight, down_weight):
-    gate = jnp.dot(rows, gate_weight, preferred_element_type=jnp.float32)
-    up = jnp.dot(rows, up_weight, preferred_element_type=jnp.float32)
-    hidden = ((up + 1.0) * gate * jax.nn.sigmoid(ALPHA * gate)).astype(jnp.bfloat16)
-    return jnp.dot(hidden, down_weight, preferred_element_type=jnp.float32).astype(jnp.bfloat16)
+def expert_kernel(tail, x_ref, gate_ref, up_ref, down_ref, out_ref, total_ref):
+    step = pl.program_id(1)
+    steps = pl.num_programs(1)
+
+    def term(valid):
+        rows = x_ref[...]
+        gate = jnp.dot(rows, gate_ref[0, :, :valid], preferred_element_type=jnp.float32)
+        up = jnp.dot(rows, up_ref[0, :, :valid], preferred_element_type=jnp.float32)
+        hidden = ((up + 1.0) * gate * jax.nn.sigmoid(ALPHA * gate)).astype(jnp.bfloat16)
+        return jnp.dot(hidden, down_ref[0, :valid, :], preferred_element_type=jnp.float32)
+
+    @pl.when(step == 0)
+    def _():
+        total_ref[...] = jnp.zeros_like(total_ref)
+
+    @pl.when(step < steps - 1)
+    def _():
+        total_ref[...] += term(CHUNK)
+
+    @pl.when(step == steps - 1)
+    def _():
+        out_ref[...] = (total_ref[...] + term(tail)).astype(out_ref.dtype)
+
+
+def expert_apply(rows, w_gate, w_up, w_down):
+    count, width = rows.shape
+    hidden = w_gate.shape[2]
+    steps = -(-hidden // CHUNK)
+    block = max(b for b in range(ROWS, min(count, 512) + 1, ROWS) if count % b == 0)
+    return pl.pallas_call(
+        functools.partial(expert_kernel, hidden - (steps - 1) * CHUNK),
+        grid=(count // block, steps),
+        in_specs=[
+            pl.BlockSpec((block, width), lambda r, f: (r, 0)),
+            pl.BlockSpec((1, width, CHUNK), lambda r, f: (0, 0, f)),
+            pl.BlockSpec((1, width, CHUNK), lambda r, f: (0, 0, f)),
+            pl.BlockSpec((1, CHUNK, width), lambda r, f: (0, f, 0)),
+        ],
+        out_specs=pl.BlockSpec((block, width), lambda r, f: (r, 0)),
+        out_shape=jax.ShapeDtypeStruct((count, width), jnp.bfloat16),
+        scratch_shapes=[pltpu.VMEM((block, width), jnp.float32)],
+        compiler_params=pltpu.CompilerParams(vmem_limit_bytes=48 * 1024 * 1024),
+        cost_estimate=pl.CostEstimate(
+            flops=6 * count * width * hidden,
+            bytes_accessed=6 * width * hidden + 4 * count * width,
+            transcendentals=count * hidden,
+        ),
+    )(rows, w_gate, w_up, w_down)
 
 
 def fold_plan(most, width):
@@ -81,7 +129,7 @@
     select, weights = routing(expert_ids, route_weights, experts, total)
     packed = jnp.dot(ordered(select), tokens, preferred_element_type=jnp.float32).astype(jnp.bfloat16)
     received = lax.all_to_all(fold(packed, *plan), AXES, split_axis=0, concat_axis=0, tiled=True)
-    produced = expert_apply(unfold(received, *plan), w_gate[0], w_up[0], w_down[0])
+    produced = expert_apply(unfold(received, *plan), w_gate, w_up, w_down)
     returned = lax.all_to_all(fold(produced, *plan), AXES, split_axis=0, concat_axis=0, tiled=True)
     mixed = lax.dot_general(
         ordered(weights), unfold(returned, *plan), (((0,), (0,)), ((), ())), preferred_element_type=jnp.float32

time: 133 us -> 122 us (0.917)
  matrix products: 37.7 us -> 3.35 us
  Pallas kernels: 0 us -> 23.2 us
    dot_general x2 -> x0, matrix products: 34.3 us -> none  [the longest x1 23.1 us: expert_apply(): jnp.dot(hidden, down_weight, preferred_element_type=jnp.float32)]
    pallas_call x0 -> x1, Pallas kernels: none -> 23.2 us  [expert_apply(): pl.pallas_call(functools.partial(expert_kernel, hidden - (steps - 1) * CH...]
where the time goes in v3:
time: 122 us; the launch traced here: 121 us
  blocking collectives  45.2 us (37%)
  waiting for transfers between devices  38.9 us (32%)
  Pallas kernels  23.2 us (19%)
  starting transfers between devices  5.61 us (5%)
  matrix products  3.35 us (3%)
  other arithmetic  2.41 us (2%)
  local copies, waits for them, and re-layouts  2.39 us (2%)
    all_to_all x1, blocking collectives, body(): lax.all_to_all(fold(packed, *plan), AXES, split_axis=0, concat_axis=0, ti...  45.2 us
    all_to_all x1, waiting for transfers between devices, body(): lax.all_to_all(fold(produced, *plan), AXES, split_axis=0, concat_axis=0,...  38.9 us
    pallas_call x1, Pallas kernels, expert_apply(): pl.pallas_call(functools.partial(expert_kernel, hidden - (steps - 1) * CH...  23.2 us
    all_to_all x1, starting transfers between devices, body(): lax.all_to_all(fold(produced, *plan), AXES, split_axis=0, concat_axis=0,...  5.61 us
    dot_general x1, matrix products, body(): lax.dot_general(ordered(weights), unfold(returned, *plan), (((0,), (0,)),...  2.63 us
  transfers between devices with their start and end apart: 1, of which 1 were waited for; matrix products, arithmetic and copies ran while one was open for 0% of the time, Pallas kernels for 0%

profile of v3, /device:TPU:15, one launch (start us, length us, event | category | flops | bytes accessed | tf_op | source)
XLA Modules:
  0.0 121.3 jit_solution(1845431072809317705)
XLA Ops:
  0.0 0.0 copy-start
  0.0 0.7 fusion.11
  0.7 0.1 convolution_convert_fusion.2
  1.0 0.0 copy-done
  1.0 0.6 convolution_convert_fusion
  1.6 0.1 slice.60
  1.8 0.1 concatenate.31
  1.9 0.1 pad.14
  2.0 0.1 pad_maximum_fusion
  2.1 45.2 %all_to_all.10 = bf16[16,16,3328]{2,1,0:T(8,128)(2,1)S(1)} all-to-all(bf16[16,16,3328]{2,1,0:T(8,128)(2,1)S(1)} %pad_maximum_fusion), channel_id=1, replica_groups=mesh['groups'=2,'site'=4,'member'=4] {'site','member'}, dimensions={0} | all-to-all | bytes 3407872 | tf_op jit(solution)/shard_map/all_to_all | solution.py:131
  47.4 0.1 slice.62
  47.5 0.1 reshape.45
  47.6 0.1 pad_maximum_fusion.2.x_ref
  47.7 23.2 %shard_map.64 = bf16[288,2880]{1,0:T(8,128)(2,1)S(1)} custom-call(bf16[288,2880]{1,0:T(8,128)(2,1)S(1)} %pad_maximum_fusion.2.x_ref, bf16[1,2880,2880]{2,1,0:T(8,128)(2,1)} %gate_ref.1, bf16[1,2880,2880]{2,1,0:T(8,128)(2,1)} %up_ref.1, bf16[1,2880,2880]{2,1,0:T(8,128)(2,1)} %down_ref.1), custom_call_target="tpu_custom_call" | custom-call | flops 14332723200 | bytes 53084160 | tf_op jit(solution)/shard_map/pallas_call | solution.py:65
  71.0 0.1 slice.65
  71.1 0.1 concatenate.35
  71.2 0.1 pad.16
  71.4 1.3 %pad_maximum_fusion.1 = bf16[16,16,3328]{2,1,0:T(8,128)(2,1)} fusion(bf16[16,16,384]{2,1,0:T(8,128)(2,1)S(1)} %concatenate.35, bf16[16,16,2944]{2,1,0:T(8,128)(2,1)S(1)} %bitcast.16), kind=kLoop, calls=%fused_computation.3 | loop fusion | flops 3407872 | bytes 3407872 | tf_op jit(solution)/shard_map/concatenate | solution.py:101
  72.7 0.0 copy-start.3
  72.7 0.0 copy-start.2
  72.7 5.6 %all-to-all-start.1 = ((bf16[16,16,3328]{2,1,0:T(8,128)(2,1)}), bf16[16,16,3328]{2,1,0:T(8,128)(2,1)S(1)}, u32[]{:S(2)}, u32[]{:S(2)}) async-start(bf16[16,16,3328]{2,1,0:T(8,128)(2,1)} %pad_maximum_fusion.1), calls=%async_computation.1 | async-start | bytes 3407872 | tf_op jit(solution)/shard_map/all_to_all | solution.py:133
  78.3 0.0 copy-done.3
  78.3 0.0 copy-done.2
  78.4 38.9 %all-to-all-done.1 = bf16[16,16,3328]{2,1,0:T(8,128)(2,1)S(1)} async-done(((bf16[16,16,3328]{2,1,0:T(8,128)(2,1)}), bf16[16,16,3328]{2,1,0:T(8,128)(2,1)S(1)}, u32[]{:S(2)}, u32[]{:S(2)}) %all-to-all-start.1) | async-done | bytes 1703968 | tf_op jit(solution)/shard_map/all_to_all | solution.py:133
  117.3 0.0 copy-start.1
  117.3 1.3 %slice.67 = bf16[256,2880]{1,0:T(8,128)(2,1)} slice(bf16[256,3328]{1,0:T(8,128)(2,1)S(1)} %bitcast.13), slice={[0:256], [0:2880]} | slice | bytes 2949120 | tf_op jit(solution)/shard_map/slice | solution.py:108
  118.6 0.1 reshape.47
  118.7 2.6 %convolution_convert_fusion.1 = bf16[64,2880]{1,0:T(8,128)(2,1)} fusion(bf16[32,2880]{1,0:T(8,128)(2,1)S(1)} %slice.69, bf16[256,2880]{1,0:T(8,128)(2,1)} %slice.67, bf16[32,64]{1,0:T(8,128)(2,1)S(1)} %bitcast.24, bf16[256,64]{1,0:T(8,128)(2,1)S(1)} %bitcast.19), kind=kOutput, calls=%fused_computation.1 | convolution fusion | flops 109744128 | bytes 2064384 | tf_op jit(solution)/shard_map/dot_general | solution.py:134
  121.3 0.0 copy-done.1
  (16 shorter events, 0.3 us)
Async XLA Ops:
  0.0 1.0 copy-start
  72.7 5.6 %copy-start.3 = (bf16[64,4]{0,1:T(4,128)(2,1)S(1)}, bf16[64,4]{0,1:T(4,128)(2,1)}, u32[]{:S(2)}) copy-start(bf16[64,4]{0,1:T(4,128)(2,1)} %param.8) | copy-start | bytes 1540
  72.7 5.6 %copy-start.2 = (s32[64,4]{0,1:T(4,128)S(1)}, s32[64,4]{0,1:T(4,128)}, u32[]{:S(2)}) copy-start(s32[64,4]{0,1:T(4,128)} %param.7) | copy-start | bytes 3076
  72.7 44.6 %all-to-all-start.1 = ((bf16[16,16,3328]{2,1,0:T(8,128)(2,1)}), bf16[16,16,3328]{2,1,0:T(8,128)(2,1)S(1)}, u32[]{:S(2)}, u32[]{:S(2)}) async-start(bf16[16,16,3328]{2,1,0:T(8,128)(2,1)} %pad_maximum_fusion.1), calls=%async_computation.1 | async-start | bytes 3407872 | tf_op jit(solution)/shard_map/all_to_all | solution.py:133
  117.3 4.0 %copy-start.1 = (bf16[64,2880]{1,0:T(8,128)(2,1)S(1)}, bf16[64,2880]{1,0:T(8,128)(2,1)}, u32[]{:S(2)}) copy-start(bf16[64,2880]{1,0:T(8,128)(2,1)} %param.6) | copy-start | bytes 1105924

commit v4 on v3

--- a/solution.py
+++ b/solution.py
@@ -110,6 +110,78 @@
     return jnp.concatenate([main, further], axis=0)
 
 
+def exchange_kernel(sites, members, src_ref, dst_ref, local_sem, send_sems, recv_sems):
+    site, member = lax.axis_index("site"), lax.axis_index("member")
+    me = site * members + member
+    count = sites * members
+
+    def place(k):
+        to_site = lax.rem(site + k // members, sites)
+        to_member = lax.rem(member + lax.rem(k, members), members)
+        return to_site, to_member
+
+    def origin(k):
+        from_site = lax.rem(site + sites - k // members, sites)
+        from_member = lax.rem(member + members - lax.rem(k, members), members)
+        return from_site * members + from_member
+
+    def copy(k, landing):
+        to_site, to_member = place(k)
+        return pltpu.make_async_remote_copy(
+            src_ref=src_ref.at[to_site * members + to_member],
+            dst_ref=dst_ref.at[landing],
+            send_sem=send_sems.at[k],
+            recv_sem=recv_sems.at[k],
+            device_id={"site": to_site, "member": to_member},
+            device_id_type=pl.DeviceIdType.MESH,
+        )
+
+    barrier = pltpu.get_barrier_semaphore()
+
+    @pl.loop(1, count)
+    def _(k):
+        to_site, to_member = place(k)
+        pl.semaphore_signal(
+            barrier, inc=1, device_id={"site": to_site, "member": to_member}, device_id_type=pl.DeviceIdType.MESH
+        )
+
+    pl.semaphore_wait(barrier, count - 1)
+
+    @pl.loop(1, count)
+    def _(k):
+        copy(count - k, me).start()
+
+    own = pltpu.make_async_copy(src_ref.at[me], dst_ref.at[me], local_sem)
+    own.start()
+    own.wait()
+
+    @pl.loop(1, count)
+    def _(k):
+        arriving = copy(k, origin(k))
+        arriving.wait_send()
+        arriving.wait_recv()
+
+
+def exchange(blocks):
+    sites, members = lax.axis_size("site"), lax.axis_size("member")
+    count = sites * members
+    return pl.pallas_call(
+        functools.partial(exchange_kernel, sites, members),
+        in_specs=[pl.BlockSpec(memory_space=pltpu.VMEM)],
+        out_specs=pl.BlockSpec(memory_space=pltpu.VMEM),
+        out_shape=jax.ShapeDtypeStruct(blocks.shape, blocks.dtype),
+        scratch_shapes=[
+            pltpu.SemaphoreType.DMA,
+            pltpu.SemaphoreType.DMA((count,)),
+            pltpu.SemaphoreType.DMA((count,)),
+        ],
+        compiler_params=pltpu.CompilerParams(
+            collective_id=0, has_side_effects=True, vmem_limit_bytes=48 * 1024 * 1024
+        ),
+        cost_estimate=pl.CostEstimate(flops=0, bytes_accessed=4 * blocks.size, transcendentals=0),
+    )(blocks)
+
+
 def body(tokens, expert_ids, route_weights, w_gate, w_up, w_down):
     experts = EXP_SITE * lax.axis_size("site")
     split = lax.axis_size("member") // EXP_SITE
@@ -128,9 +200,9 @@
 
     select, weights = routing(expert_ids, route_weights, experts, total)
     packed = jnp.dot(ordered(select), tokens, preferred_element_type=jnp.float32).astype(jnp.bfloat16)
-    received = lax.all_to_all(fold(packed, *plan), AXES, split_axis=0, concat_axis=0, tiled=True)
+    received = exchange(fold(packed, *plan))
     produced = expert_apply(unfold(received, *plan), w_gate, w_up, w_down)
-    returned = lax.all_to_all(fold(produced, *plan), AXES, split_axis=0, concat_axis=0, tiled=True)
+    returned = exchange(fold(produced, *plan))
     mixed = lax.dot_general(
         ordered(weights), unfold(returned, *plan), (((0,), (0,)), ((), ())), preferred_element_type=jnp.float32
     )

time: 122 us -> 114 us (0.934)
  the two profiles are of different devices: /device:TPU:15 before, /device:TPU:0 now
where the time goes in v4:
time: 114 us
  Pallas kernels  109 us (96%)
  matrix products  1.96 us (2%)
  local copies, waits for them, and re-layouts  1.77 us (2%)
  other arithmetic  1.22 us (1%)
    pallas_call x2, Pallas kernels, exchange(): pl.pallas_call(functools.partial(exchange_kernel, sites, members), in_spe...  85.7 us
    pallas_call x1, Pallas kernels, expert_apply(): pl.pallas_call(functools.partial(expert_kernel, hidden - (steps - 1) * CH...  23.2 us

profile of v4, /device:TPU:0, one launch (start us, length us, event | category | flops | bytes accessed | tf_op | source)
XLA Modules:
  0.0 114.2 jit_solution(9643567838955066955)
XLA Ops:
  0.0 0.0 copy-start
  0.0 0.7 fusion.11
  0.7 0.1 convolution_convert_fusion.2
  1.0 0.0 copy-done
  1.0 0.6 convolution_convert_fusion
  1.6 0.1 concatenate.31
  1.7 0.1 slice.60
  1.9 0.1 pad.14
  2.0 0.1 pad_maximum_fusion.src_ref
  2.1 44.7 %shard_map.64 = bf16[16,16,3328]{2,1,0:T(8,128)(2,1)S(1)} custom-call(bf16[16,16,3328]{2,1,0:T(8,128)(2,1)S(1)} %pad_maximum_fusion.src_ref), custom_call_target="tpu_custom_call" | custom-call | bytes 3407872 | tf_op jit(solution)/shard_map/pallas_call | solution.py:168
  46.9 0.1 reshape.45
  47.0 0.1 slice.62
  47.1 0.1 pad_maximum_fusion.2.x_ref
  47.2 23.2 %shard_map.65 = bf16[288,2880]{1,0:T(8,128)(2,1)S(1)} custom-call(bf16[288,2880]{1,0:T(8,128)(2,1)S(1)} %pad_maximum_fusion.2.x_ref, bf16[1,2880,2880]{2,1,0:T(8,128)(2,1)} %gate_ref.1, bf16[1,2880,2880]{2,1,0:T(8,128)(2,1)} %up_ref.1, bf16[1,2880,2880]{2,1,0:T(8,128)(2,1)} %down_ref.1), custom_call_target="tpu_custom_call" | custom-call | flops 14332723200 | bytes 53084160 | tf_op jit(solution)/shard_map/pallas_call | solution.py:65
  70.5 0.1 concatenate.35
  70.6 0.1 slice.65
  70.7 0.1 pad.16
  70.9 0.1 pad_maximum_fusion.1.src_ref
  71.0 41.0 %shard_map.66 = bf16[16,16,3328]{2,1,0:T(8,128)(2,1)S(1)} custom-call(bf16[16,16,3328]{2,1,0:T(8,128)(2,1)S(1)} %pad_maximum_fusion.1.src_ref), custom_call_target="tpu_custom_call" | custom-call | bytes 3407872 | tf_op jit(solution)/shard_map/pallas_call | solution.py:168
  112.0 0.1 reshape.47
  112.1 0.0 copy-start.3
  112.1 0.0 copy-start.2
  112.2 0.0 copy-start.1
  112.2 0.1 slice.67
  112.3 0.5 copy-done.3
  112.8 0.0 copy-done.2
  112.8 0.1 select_convert_fusion
  112.9 1.3 %convolution_convert_fusion.1 = bf16[64,2880]{1,0:T(8,128)(2,1)} fusion(bf16[32,2880]{1,0:T(8,128)(2,1)S(1)} %slice.69, bf16[256,2880]{1,0:T(8,128)(2,1)S(1)} %slice.67, bf16[32,64]{1,0:T(8,128)(2,1)S(1)} %bitcast.24, bf16[256,64]{1,0:T(8,128)(2,1)S(1)} %bitcast.19), kind=kOutput, calls=%fused_computation.1 | convolution fusion | flops 109744128 | bytes 2064384 | tf_op jit(solution)/shard_map/dot_general | solution.py:206
  114.2 0.0 copy-done.1
  (15 shorter events, 0.2 us)
Async XLA Ops:
  0.0 1.0 copy-start
  112.1 0.7 copy-start.3
  112.1 0.7 copy-start.2
  112.2 2.0 %copy-start.1 = (bf16[64,2880]{1,0:T(8,128)(2,1)S(1)}, bf16[64,2880]{1,0:T(8,128)(2,1)}, u32[]{:S(2)}) copy-start(bf16[64,2880]{1,0:T(8,128)(2,1)} %param.6) | copy-start | bytes 1105924
